TPU v7x, 32 devices: a whole 2x2x4 slice. The times are simulated.
32 devices in a mesh: region: 16 (over z, y, x), sub: 2 (over core).
Axes of the slice: x: 2, y: 2, z: 4, core: 2. Of those that a mesh axis runs over, the one named last changes fastest.
Arguments:
- probes: float32 [32768, 128], P(('region', 'sub')), may hold values from -6 to 6
- neighbours: int32 [32768, 8], P(('region', 'sub')), may hold values from 0 to 1535, as said below
- lengths: int32 [32768, 8], P(('region', 'sub')), may hold values from 0 to 999, as said below
- iid_precision: float32 [32768], P(('region', 'sub')), may hold values from 0.1 to 2
- send_rows: int32 [64, 256], P(('region', 'sub')), may hold values from 0 to 1023, as said below
Outputs:
- solution: float32 [32768, 128], P(('region', 'sub'))
- trace_terms: float32 [128], replicated
Inputs may be any that keep to these rules, and one draw needn't show every extreme that they name: `neighbours`: slots 0 to 5 name rows of the same device; slot 6 names 1024 + b for the b-th row received from device d - 1 or the block itself, slot 7 names 1280 + b for the b-th row received from device d + 1 or the block itself. The weighted links are symmetric across the whole grid, and the first and last devices have no links across their outer side. `lengths`: A slot that names its own block has length 0. `send_rows`: the entries of each row are distinct.
All inputs are finite; a program needn't handle non-finite values.
Results may differ from a plain program's by a relative error of at most 0.0003.
Values sent between devices are 32-bit elements; how exact they have to be, the bound alone decides.
A program may use at most 64 MiB of HBM per device.

v0:
```python
import jax
import jax.numpy as jnp
from jax import lax
from jax.sharding import PartitionSpec as P

ITERS = 3
GROUP = 8


metres_unit = 1000.0


def passed_along(shard, axis, by):
    size = lax.axis_size(axis)
    pairs = [(i, i + by) for i in range(size) if 0 <= i + by < size]
    return lax.ppermute(shard, axis, pairs)


def apply_rows(own, extended, neighbours, weights, center):
    total = center[:, None] * own
    for slot in range(neighbours.shape[1]):
        total = total - weights[:, slot, None] * extended[neighbours[:, slot]]
    return total


def block_inverses(neighbours, weights, center):
    count = neighbours.shape[0]
    index = jnp.arange(count, dtype=jnp.int32)
    columns = (index // GROUP * GROUP)[:, None] + jnp.arange(GROUP, dtype=jnp.int32)[None, :]
    hits = (neighbours[:, :, None] == columns[:, None, :]).astype(jnp.float32)
    offdiag = -jnp.sum(weights[:, :, None] * hits, axis=1)
    ondiag = center[:, None] * (columns == index[:, None]).astype(jnp.float32)
    blocks = (offdiag + ondiag).reshape(count // GROUP, GROUP, GROUP)
    factor = jnp.linalg.cholesky(blocks)
    identity = jnp.broadcast_to(jnp.eye(GROUP, dtype=jnp.float32), blocks.shape)
    lower = lax.linalg.triangular_solve(factor, identity, left_side=True, lower=True)
    return lax.linalg.triangular_solve(factor, lower, left_side=True, lower=True, transpose_a=True)


def precondition(inverse, residual):
    grouped = residual.reshape(inverse.shape[0], GROUP, residual.shape[1])
    return jnp.einsum("gij,gjp->gip", inverse, grouped, precision=lax.Precision.HIGHEST).reshape(
        residual.shape
    )


def extended_rows(field, send_rows):
    from_left = passed_along(field[send_rows[1]], ("region", "sub"), 1)
    from_right = passed_along(field[send_rows[0]], ("region", "sub"), -1)
    return jnp.concatenate([field, from_left, from_right], axis=0)


def residual_norm(residual, precond):
    return lax.psum(jnp.sum(residual * precond, axis=0), ("region", "sub"))


def direction_curvature(direction, image):
    terms = (jnp.sum(direction * image, axis=0),)
    return lax.psum((terms[0],), ("region", "sub"))


def on_device(probes, neighbours, lengths, iid_precision, send_rows):
    weights = lengths.astype(jnp.float32) / metres_unit
    links = jnp.sum(weights, axis=1)
    center = links + iid_precision
    inverse = block_inverses(neighbours, weights, center)
    cells = probes.shape[0] * lax.axis_size("region") * lax.axis_size("sub")

    def operate(field, diagonal):
        return apply_rows(field, extended_rows(field, send_rows), neighbours, weights, diagonal)

    laplace = operate(probes, links)
    solution = jnp.zeros_like(probes)
    residual = probes
    precond = precondition(inverse, residual)
    direction = precond
    gamma = residual_norm(residual, precond)
    for step in range(ITERS):
        image = operate(direction, center)
        sums = direction_curvature(direction, image)
        alpha = gamma / sums[0]
        solution = solution + alpha * direction
        if step + 1 < ITERS:
            residual = residual - alpha * image
            precond = precondition(inverse, residual)
            gamma_new = residual_norm(residual, precond)
            direction = precond + gamma_new / gamma * direction
            gamma = gamma_new
    totals = lax.psum(jnp.sum(solution * laplace, axis=0), ("region", "sub"))
    return (solution, totals / cells)


def solution(mesh):
    return jax.shard_map(
        on_device,
        mesh=mesh,
        in_specs=(
            P(("region", "sub"), None),
            P(("region", "sub"), None),
            P(("region", "sub"), None),
            P(("region", "sub")),
            P(("region", "sub"), None),
        ),
        out_specs=(P(("region", "sub"), None), P()),
        check_vma=False,
    )
```

profile of v0, /device:TPU:15, one launch (start us, length us, event | category | flops | bytes accessed | tf_op | source)
XLA Modules:
  0.0 552.3 jit_solution(14099944614176837604)
XLA Ops:
  4.3 93.9 %custom-call.9 = f32[128,8,8]{2,1,0:T(8,128)S(1)} custom-call(f32[128,8,8]{2,1,0:T(8,128)S(1)} %copy.37), custom_call_target="Cholesky" | custom-call | tf_op jit(solution)/shard_map/jit(cholesky)/cholesky | solution.py:34
  99.7 1.2 fusion.38
  100.9 1.0 fusion.49
  101.9 1.5 multiply_reduce_fusion.1
  104.1 3.7 collective-permute-start
  108.6 1.9 collective-permute-start.1
  117.6 4.0 gather_fusion.2
  121.6 4.0 gather_fusion.3
  125.6 4.0 gather_fusion.4
  129.6 4.0 gather_fusion.5
  133.7 4.0 gather_fusion.6
  137.7 4.0 gather_fusion.7
  141.7 4.0 gather_fusion.8
  145.7 4.0 gather_fusion.9
  149.8 4.5 fusion.28
  154.2 40.8 %all-reduce = (f32[128]{0:T(128)}, f32[128]{0:T(128)}) all-reduce(f32[128]{0:T(128)} %get-tuple-element.14, f32[128]{0:T(128)} %fusion.28), channel_id=1, replica_groups=mesh['region'=16,'sub'=2] {'region','sub'}, use_global_device_ids=true, to_apply=%region_5.6 | all-reduce | flops 256 | bytes 2048 | tf_op jit(solution)/shard_map/psum | solution.py:54
  196.4 3.7 multiply_subtract_fusion.1
  200.1 1.0 fusion.23
  201.1 39.1 %psum.51 = f32[128]{0:T(128)S(1)} all-reduce(f32[128]{0:T(128)S(1)} %get-tuple-element.37), channel_id=1, replica_groups=mesh['region'=16,'sub'=2] {'region','sub'}, use_global_device_ids=true, to_apply=%region_9.10 | all-reduce | flops 128 | bytes 1024 | tf_op jit(solution)/shard_map/psum | solution.py:54
  242.9 4.3 collective-permute-start.2
  247.3 1.9 collective-permute-start.3
  249.2 1.3 gather_fusion.30
  250.5 5.4 collective-permute-start.6
  256.0 1.3 gather_fusion.31
  257.3 2.1 collective-permute-start.7
  259.5 4.0 gather_fusion.12
  263.5 4.0 gather_fusion.13
  267.5 4.0 gather_fusion.14
  271.5 4.0 gather_fusion.15
  275.5 4.0 gather_fusion.16
  279.6 4.0 gather_fusion.17
  283.6 4.0 gather_fusion.18
  287.6 4.0 gather_fusion.19
  291.6 4.1 fusion.15
  295.8 40.3 %psum.52 = f32[128]{0:T(128)S(1)} all-reduce(f32[128]{0:T(128)S(1)} %fusion.15), channel_id=1, replica_groups=mesh['region'=16,'sub'=2] {'region','sub'}, use_global_device_ids=true, to_apply=%region_11.12 | all-reduce | flops 128 | bytes 1024 | tf_op jit(solution)/shard_map/psum | solution.py:59
  336.1 7.5 %fusion.10 = (f32[128]{0:T(128)}, f32[128,8,128]{2,1,0:T(8,128)S(1)}) fusion(f32[128,8,8]{2,1,0:T(8,128)S(1)} %copy-done.2, f32[1024,128]{1,0:T(8,128)} %copy-done.5, f32[1024,128]{1,0:T(8,128)} %gather_fusion.19, f32[1024]{0:T(1024)} %bitcast.246, f32[1024,128]{1,0:T(8,128)} %gather_fusion.18, f32[1024]{0:T(1024)} %bitcast.224, ...), kind=kOutput, calls=%fused_computation.63 | convolution fusion | flops 17825664 | bytes 5837824 | tf_op jit(solution)/shard_map/gij,gjp->gip/dot_general | solution.py:42
  344.2 39.1 %psum.53 = f32[128]{0:T(128)S(1)} all-reduce(f32[128]{0:T(128)S(1)} %copy-done.55), channel_id=1, replica_groups=mesh['region'=16,'sub'=2] {'region','sub'}, use_global_device_ids=true, to_apply=%region_13.14 | all-reduce | flops 128 | bytes 1024 | tf_op jit(solution)/shard_map/psum | solution.py:54
  384.4 1.5 gather_fusion.20
  385.9 1.5 gather_fusion.21
  387.4 4.1 collective-permute-start.4
  391.5 2.0 collective-permute-start.5
  393.6 0.9 constant_dynamic-update-slice_fusion.1
  394.5 0.9 constant_dynamic-update-slice_fusion
  395.4 4.0 gather_fusion.32
  399.5 4.0 gather_fusion.33
  403.5 4.0 gather_fusion.34
  407.5 4.0 gather_fusion.35
  411.5 4.3 gather_fusion.36
  415.9 4.3 gather_fusion.37
  420.2 4.3 gather_fusion.38
  424.6 4.3 gather_fusion.39
  428.9 1.0 pad_maximum_fusion.2
  429.9 4.0 gather_fusion.22
  434.0 4.0 gather_fusion.23
  438.0 4.0 gather_fusion.24
  442.0 4.0 gather_fusion.25
  446.1 4.0 gather_fusion.26
  450.1 4.0 gather_fusion.27
  454.1 4.0 gather_fusion.28
  458.2 4.1 gather_fusion.29
  462.3 3.9 fusion.2
  466.3 40.3 %psum.54 = f32[128]{0:T(128)S(1)} all-reduce(f32[128]{0:T(128)S(1)} %fusion.2), channel_id=1, replica_groups=mesh['region'=16,'sub'=2] {'region','sub'}, use_global_device_ids=true, to_apply=%region_15.16 | all-reduce | flops 128 | bytes 1024 | tf_op jit(solution)/shard_map/psum | solution.py:59
  507.3 4.6 multiply_reduce_fusion
  511.8 39.9 %psum.55 = f32[128]{0:T(128)S(1)} all-reduce(f32[128]{0:T(128)S(1)} %get-tuple-element.12), channel_id=1, replica_groups=mesh['region'=16,'sub'=2] {'region','sub'}, use_global_device_ids=true, to_apply=%region_17.18 | all-reduce | flops 128 | bytes 1024 | tf_op jit(solution)/shard_map/psum | solution.py:89
  (189 shorter events, 20.5 us)
Async XLA Ops:
  0.7 0.8 copy-start.49
  2.7 0.8 copy-start.9
  100.8 1.0 copy-start.52
  100.9 1.0 copy-start
  101.8 98.3 %copy-start.1 = (f32[128,8,8]{2,1,0:T(8,128)}, f32[128,8,8]{2,1,0:T(8,128)S(1)}, u32[]{:S(2)}) copy-start(f32[128,8,8]{2,1,0:T(8,128)S(1)} %fusion.49) | copy-start | bytes 98308
  103.4 0.7 copy-start.43
  103.4 4.4 copy-start.41
  104.1 13.4 %collective-permute-start = (f32[256,128]{1,0:T(8,128)S(1)}, f32[256,128]{1,0:T(8,128)S(1)}, u32[]{:S(2)}, u32[]{:S(2)}) collective-permute-start(f32[256,128]{1,0:T(8,128)S(1)} %gather_fusion), channel_id=1, source_target_pairs={{0,1},{1,2},{2,3},{3,4},{4,5},{5,6},{6,7},{7,8},{8,9},{9,10},{10,1... | collective-permute-start | bytes 393224 | tf_op jit(solution)/shard_map/ppermute | solution.py:16
  108.6 8.9 %collective-permute-start.1 = (f32[256,128]{1,0:T(8,128)S(1)}, f32[256,128]{1,0:T(8,128)S(1)}, u32[]{:S(2)}, u32[]{:S(2)}) collective-permute-start(f32[256,128]{1,0:T(8,128)S(1)} %gather_fusion.1), channel_id=1, source_target_pairs={{1,0},{2,1},{3,2},{4,3},{5,4},{6,5},{7,6},{8,7},{9,8},{10,9},{11,1... | collective-permute-start | bytes 393224 | tf_op jit(solution)/shard_map/ppermute | solution.py:16
  129.6 4.0 copy-start.13
  133.6 4.0 copy-start.10
  137.7 4.0 copy-start.19
  141.7 4.0 copy-start.16
  149.7 46.5 %copy-start.6 = (f32[1024,128]{1,0:T(8,128)S(1)}, f32[1024,128]{1,0:T(8,128)}, u32[]{:S(2)}) copy-start(f32[1024,128]{1,0:T(8,128)} %gather_fusion.2) | copy-start | bytes 1572868
  149.7 46.5 %copy-start.7 = (f32[1024,128]{1,0:T(8,128)S(1)}, f32[1024,128]{1,0:T(8,128)}, u32[]{:S(2)}) copy-start(f32[1024,128]{1,0:T(8,128)} %gather_fusion.3) | copy-start | bytes 1572868
  195.0 0.7 copy-start.61
  195.0 0.7 copy-start.63
  195.6 0.7 copy-start.36
  195.7 0.7 copy-start.34
  195.7 0.7 copy-start.32
  195.7 0.7 copy-start.30
  195.7 0.7 copy-start.28
  195.7 0.7 copy-start.26
  195.7 0.7 copy-start.24
  195.7 0.7 copy-start.23
  200.1 1.0 copy-start.5
  201.1 39.7 %copy-start.3 = (f32[128,8,128]{2,1,0:T(8,128)}, f32[128,8,128]{2,1,0:T(8,128)S(1)}, u32[]{:S(2)}) copy-start(f32[128,8,128]{2,1,0:T(8,128)S(1)} %get-tuple-element.38) | copy-start | bytes 1572868
  201.1 39.2 %copy-start.62 = (f32[128]{0:T(128)S(1)}, f32[128]{0:T(128)}, u32[]{:S(2)}) copy-start(f32[128]{0:T(128)} %get-tuple-element.10) | copy-start | bytes 1540
  240.8 0.7 copy-start.44
  241.5 0.7 copy-start.42
  242.9 16.5 %collective-permute-start.2 = (f32[256,128]{1,0:T(8,128)S(1)}, f32[256,128]{1,0:T(8,128)S(1)}, u32[]{:S(2)}, u32[]{:S(2)}) collective-permute-start(f32[256,128]{1,0:T(8,128)S(1)} %gather_fusion.10), channel_id=1, source_target_pairs={{0,1},{1,2},{2,3},{3,4},{4,5},{5,6},{6,7},{7,8},{8,9},{9,10},{10,1... | collective-permute-start | bytes 393224 | tf_op jit(solution)/shard_map/ppermute | solution.py:16
  247.3 12.2 %collective-permute-start.3 = (f32[256,128]{1,0:T(8,128)S(1)}, f32[256,128]{1,0:T(8,128)S(1)}, u32[]{:S(2)}, u32[]{:S(2)}) collective-permute-start(f32[256,128]{1,0:T(8,128)S(1)} %gather_fusion.11), channel_id=1, source_target_pairs={{1,0},{2,1},{3,2},{4,3},{5,4},{6,5},{7,6},{8,7},{9,8},{10,9},{11,1... | collective-permute-start | bytes 393224 | tf_op jit(solution)/shard_map/ppermute | solution.py:16
  250.5 143.1 %collective-permute-start.6 = (f32[256,128]{1,0:T(8,128)}, f32[256,128]{1,0:T(8,128)}, u32[]{:S(2)}, u32[]{:S(2)}) collective-permute-start(f32[256,128]{1,0:T(8,128)} %gather_fusion.30), channel_id=1, source_target_pairs={{0,1},{1,2},{2,3},{3,4},{4,5},{5,6},{6,7},{7,8},{8,9},{9,10},{10,1... | collective-permute-start | bytes 393224 | tf_op jit(solution)/shard_map/ppermute | solution.py:16
  257.3 137.2 %collective-permute-start.7 = (f32[256,128]{1,0:T(8,128)}, f32[256,128]{1,0:T(8,128)}, u32[]{:S(2)}, u32[]{:S(2)}) collective-permute-start(f32[256,128]{1,0:T(8,128)} %gather_fusion.31), channel_id=1, source_target_pairs={{1,0},{2,1},{3,2},{4,3},{5,4},{6,5},{7,6},{8,7},{9,8},{10,9},{11,1... | collective-permute-start | bytes 393224 | tf_op jit(solution)/shard_map/ppermute | solution.py:16
  271.5 4.0 copy-start.14
  275.5 4.0 copy-start.11
  279.6 4.0 copy-start.20
  283.6 4.0 copy-start.17
  291.6 44.5 %copy-start.2 = (f32[128,8,8]{2,1,0:T(8,128)S(1)}, f32[128,8,8]{2,1,0:T(8,128)}, u32[]{:S(2)}) copy-start(f32[128,8,8]{2,1,0:T(8,128)} %copy-done.1) | copy-start | bytes 98308
  295.8 40.3 %copy-start.59 = (f32[128]{0:T(128)S(1)}, f32[128]{0:T(128)}, u32[]{:S(2)}) copy-start(f32[128]{0:T(128)} %copy-done.58) | copy-start | bytes 1540
  336.1 7.5 %copy-start.50 = (f32[128]{0:T(128)}, f32[128]{0:T(128)S(1)}, u32[]{:S(2)}) copy-start(f32[128]{0:T(128)S(1)} %div.57) | copy-start | bytes 1540
  343.6 0.6 copy-start.55
  344.2 39.1 %copy-start.60 = (f32[128]{0:T(128)S(1)}, f32[128]{0:T(128)}, u32[]{:S(2)}) copy-start(f32[128]{0:T(128)} %copy-done.58) | copy-start | bytes 1540
  387.4 41.5 %collective-permute-start.4 = (f32[256,128]{1,0:T(8,128)}, f32[256,128]{1,0:T(8,128)}, u32[]{:S(2)}, u32[]{:S(2)}) collective-permute-start(f32[256,128]{1,0:T(8,128)} %gather_fusion.20), channel_id=1, source_target_pairs={{0,1},{1,2},{2,3},{3,4},{4,5},{5,6},{6,7},{7,8},{8,9},{9,10},{10,1... | collective-permute-start | bytes 393224 | tf_op jit(solution)/shard_map/ppermute | solution.py:16
  391.5 37.4 %collective-permute-start.5 = (f32[256,128]{1,0:T(8,128)}, f32[256,128]{1,0:T(8,128)}, u32[]{:S(2)}, u32[]{:S(2)}) collective-permute-start(f32[256,128]{1,0:T(8,128)} %gather_fusion.21), channel_id=1, source_target_pairs={{1,0},{2,1},{3,2},{4,3},{5,4},{6,5},{7,6},{8,7},{9,8},{10,9},{11,1... | collective-permute-start | bytes 393224 | tf_op jit(solution)/shard_map/ppermute | solution.py:16
  442.0 4.0 copy-start.15
  446.1 4.0 copy-start.12
  450.1 4.0 copy-start.21
  454.1 4.0 copy-start.18
  458.1 4.1 copy-start.4
  458.1 4.1 copy-start.46
  458.2 4.1 copy-start.48
  462.2 44.4 %copy-start.8 = (f32[1024,128]{1,0:T(8,128)S(1)}, f32[1024,128]{1,0:T(8,128)}, u32[]{:S(2)}) copy-start(f32[1024,128]{1,0:T(8,128)} %gather_fusion.32) | copy-start | bytes 1572868
  462.3 44.4 %copy-start.25 = (f32[1024,1]{0,1:T(1,128)S(1)}, f32[1024,1]{0,1:T(1,128)}, u32[]{:S(2)}) copy-start(f32[1024,1]{0,1:T(1,128)} %get-tuple-element.16) | copy-start | bytes 12292
  462.3 44.4 %copy-start.27 = (f32[1024,1]{0,1:T(1,128)S(1)}, f32[1024,1]{0,1:T(1,128)}, u32[]{:S(2)}) copy-start(f32[1024,1]{0,1:T(1,128)} %get-tuple-element.17) | copy-start | bytes 12292
  462.3 44.4 %copy-start.29 = (f32[1024,1]{0,1:T(1,128)S(1)}, f32[1024,1]{0,1:T(1,128)}, u32[]{:S(2)}) copy-start(f32[1024,1]{0,1:T(1,128)} %get-tuple-element.18) | copy-start | bytes 12292
  462.3 44.4 %copy-start.31 = (f32[1024,1]{0,1:T(1,128)S(1)}, f32[1024,1]{0,1:T(1,128)}, u32[]{:S(2)}) copy-start(f32[1024,1]{0,1:T(1,128)} %get-tuple-element.19) | copy-start | bytes 12292
  462.3 44.4 %copy-start.33 = (f32[1024,1]{0,1:T(1,128)S(1)}, f32[1024,1]{0,1:T(1,128)}, u32[]{:S(2)}) copy-start(f32[1024,1]{0,1:T(1,128)} %get-tuple-element.20) | copy-start | bytes 12292
  462.3 44.4 %copy-start.35 = (f32[1024,1]{0,1:T(1,128)S(1)}, f32[1024,1]{0,1:T(1,128)}, u32[]{:S(2)}) copy-start(f32[1024,1]{0,1:T(1,128)} %get-tuple-element.21) | copy-start | bytes 12292
  462.3 44.4 %copy-start.37 = (f32[1024,1]{0,1:T(1,128)S(1)}, f32[1024,1]{0,1:T(1,128)}, u32[]{:S(2)}) copy-start(f32[1024,1]{0,1:T(1,128)} %get-tuple-element.22) | copy-start | bytes 12292
  462.3 44.4 %copy-start.38 = (f32[1024,1]{0,1:T(1,128)S(1)}, f32[1024,1]{0,1:T(1,128)}, u32[]{:S(2)}) copy-start(f32[1024,1]{0,1:T(1,128)} %get-tuple-element.23) | copy-start | bytes 12292
  462.3 44.4 %copy-start.40 = (f32[1024]{0:T(1024)S(1)}, f32[1024]{0:T(1024)}, u32[]{:S(2)}) copy-start(f32[1024]{0:T(1024)} %copy-done.39) | copy-start | bytes 12292
  466.3 40.3 %copy-start.57 = (f32[128]{0:T(128)S(1)}, f32[128]{0:T(128)}, u32[]{:S(2)}) copy-start(f32[128]{0:T(128)} %copy-done.56) | copy-start | bytes 1540
  506.6 0.7 copy-start.54
  (8 other events, 4.4 us)
where the time goes:
time: 557 us; the launch traced here: 552 us
  blocking collectives  240 us (43%)
  local copies, waits for them, and re-layouts  154 us (28%)
  other arithmetic  120 us (22%)
  starting transfers between devices  25.5 us (5%)
  matrix products  12.1 us (2%)
    gather x32, local copies, waits for them, and re-layouts, apply_rows(): total = total - weights[:, slot, None] * extended[neighbours[:, slot]]  130 us
    psum x3, blocking collectives, residual_norm(): return lax.psum(jnp.sum(residual * precond, axis=0), ('region', 'sub'))  119 us
    another operation x4, other arithmetic, block_inverses(): factor = jnp.linalg.cholesky(blocks)  94.1 us
    psum x2, blocking collectives, direction_curvature(): return lax.psum((terms[0],), ('region', 'sub'))  80.6 us
    psum x1, blocking collectives, on_device(): totals = lax.psum(jnp.sum(solution * laplace, axis=0), ('region', 'sub'))  39.9 us
    ppermute x8, starting transfers between devices, passed_along(): return lax.ppermute(shard, axis, pairs)  25.5 us
    reduce_sum x3, other arithmetic, direction_curvature(): terms = (jnp.sum(direction * image, axis=0),)  12.5 us
  transfers between devices with their start and end apart: 8, of which 0 were waited for; matrix products, arithmetic and copies ran while one was open for 17% of the time, Pallas kernels for 0%

commit v1 on v0

v1 whole, which is shorter than its diff:
```python
import functools

import jax
import jax.numpy as jnp
from jax import lax
from jax.experimental import pallas as pl
from jax.experimental.pallas import tpu as pltpu
from jax.sharding import PartitionSpec as P

GROUP = 8
STEPS = 3
UNIT = 1000.0
BLOCK = 256
LANES = 128
STATS = 16
TINY = 2e-7
F32 = jnp.float32
BF16 = jnp.bfloat16
MESH = pl.DeviceIdType.MESH


def dot(a, b):
    return jnp.dot(a, b, preferred_element_type=F32)


def split(value):
    high = value.astype(BF16)
    return high, (value - high.astype(F32)).astype(BF16)


def halves(value):
    return jnp.concatenate(split(value), axis=1)


def folded(wide):
    half = wide.shape[1] // 2
    return wide[:, :half] + wide[:, half:]


def block_inverse(block):
    lane = lax.broadcasted_iota(jnp.int32, block.shape, 1)
    sub = lax.broadcasted_iota(jnp.int32, block.shape, 0)
    place = lane % GROUP
    for p in range(GROUP):
        col = jnp.take_along_axis(block, lane - place + p, axis=1)
        inv = 1.0 / col[p : p + 1, :]
        row = block[p : p + 1, :] * inv
        rest = block - col * row
        rest = jnp.where(place == p, -col * inv, rest)
        at_row = jnp.where(place[:1] == p, inv, row)
        block = jnp.where(sub == p, at_row, rest)
    return block


def column_sum(value):
    rows, width = value.shape
    return jnp.sum(value.reshape(rows // 8, 8, width).sum(axis=0), axis=0, keepdims=True)


def kernel(
    region, inner,
    nbr_ref, len_ref, iid_ref, send_ref, b_ref,
    x_ref, trace_ref,
    ahi, alo, chi, clo, scat, bdhi, bdlo, off, wide, loc, w, a,
    ysend, yrecv, stats, gathered,
    halo_send, halo_recv, stat_send, stat_recv,
):
    rows, probes = b_ref.shape
    bound = send_ref.shape[1]
    n = region * inner
    me = lax.axis_index("region") * inner + lax.axis_index("sub")

    def device(k):
        return (k // inner, k % inner)

    barrier = pltpu.get_barrier_semaphore()

    def greet(k, carry):
        other = lax.rem(me + k, n)
        pl.semaphore_signal(barrier, inc=1, device_id=device(other), device_id_type=MESH)
        return carry

    lax.fori_loop(1, n, greet, 0)

    def halo(step, side):
        return pltpu.make_async_remote_copy(
            src_ref=ysend.at[step, side],
            dst_ref=yrecv.at[step, side],
            send_sem=halo_send.at[step, side],
            recv_sem=halo_recv.at[step, side],
            device_id=device(lax.rem(me + (1 if side == 0 else n - 1), n)),
            device_id_type=MESH,
        )

    has_next, has_prev = me < n - 1, me > 0

    @pl.when(jnp.logical_not(has_prev))
    def _():
        for step in range(STEPS):
            yrecv[step, 0] = jnp.zeros((bound, probes), F32)

    @pl.when(jnp.logical_not(has_next))
    def _():
        for step in range(STEPS):
            yrecv[step, 1] = jnp.zeros((bound, probes), F32)

    lengths = len_ref[...]
    neighbours = nbr_ref[...]
    weights = lengths.astype(F32) / UNIT
    center = jnp.sum(weights, axis=0, keepdims=True) + iid_ref[...]
    lane = lax.broadcasted_iota(jnp.int32, neighbours.shape, 1)
    sub = lax.broadcasted_iota(jnp.int32, neighbours.shape, 0)
    column = lane - lane % GROUP + sub
    blocks = jnp.where(column == lane, center, 0.0)
    for slot in range(neighbours.shape[0]):
        hit = neighbours[slot : slot + 1] == column
        blocks = blocks - jnp.where(hit, weights[slot : slot + 1], 0.0)
    inside = neighbours // GROUP == lane // GROUP
    off[...] = jnp.where(inside, 0, lengths).astype(F32)
    inverse = jnp.concatenate(
        [block_inverse(blocks[:, s : s + LANES]) for s in range(0, rows, LANES)], axis=1
    )
    across = lax.broadcasted_iota(jnp.int32, (BLOCK, BLOCK), 1) // GROUP
    down = lax.broadcasted_iota(jnp.int32, (BLOCK, BLOCK), 0) // GROUP
    for s in range(0, rows, BLOCK):
        tiled = jnp.concatenate([inverse[:, s : s + BLOCK]] * (BLOCK // GROUP), axis=0)
        bdhi[s : s + BLOCK], bdlo[s : s + BLOCK] = split(jnp.where(across == down, tiled, 0.0))

    def precondition(value_ref, out_ref):
        for s in range(0, rows, BLOCK):
            at = slice(s, s + BLOCK)
            part = halves(value_ref[at])
            out = folded(dot(bdhi[at], part) + dot(bdlo[at], part))
            out_ref[at] = out
            wide[at] = halves(out)

    for side in range(2):
        slot = 7 - side
        high, low = split(len_ref[slot : slot + 1].astype(F32))
        high, low = high.astype(F32), low.astype(F32)
        first = rows + (bound if side == 0 else 0)
        named = lax.broadcasted_iota(jnp.int32, (bound, rows), 0) + first
        hit = nbr_ref[slot : slot + 1] == named
        at = slice(side * bound, (side + 1) * bound)
        chi[at] = jnp.where(hit, high, 0.0).astype(BF16)
        clo[at] = jnp.where(hit, low, 0.0).astype(BF16)

    def send(step):
        for side in range(2):
            at = slice(side * bound, (side + 1) * bound)
            ysend[step, side] = folded(dot(chi[at], wide[...]) + dot(clo[at], wide[...]))

            @pl.when(has_next if side == 0 else has_prev)
            def _():
                halo(step, side).start()

    def build():
        for side in range(2):
            own = lax.broadcasted_iota(jnp.int32, (rows, bound), 0)
            hit = own == send_ref[side : side + 1]
            scat[:, side * bound : (side + 1) * bound] = jnp.where(hit, 1.0, 0.0).astype(BF16)

        def body(i, carry):
            start = pl.multiple_of(i * 16, 16)
            for s in range(0, rows, BLOCK):
                at = slice(s, s + BLOCK)
                named = lax.broadcasted_iota(jnp.int32, (16, BLOCK), 0) + start
                total = jnp.zeros((16, BLOCK), F32)
                for slot in range(6):
                    hit = nbr_ref[slot : slot + 1, at] == named
                    total = total + jnp.where(hit, off[slot : slot + 1, at], 0.0)
                high, low = split(total)
                ahi[pl.ds(start, 16), at] = high
                alo[pl.ds(start, 16), at] = low
            return carry

        lax.fori_loop(0, rows // 16, body, 0)

    def local():
        def body(i, carry):
            at = pl.ds(pl.multiple_of(i * BLOCK, BLOCK), BLOCK)
            loc[at] = folded(dot(ahi[at], wide[...]) + dot(alo[at], wide[...]))
            return carry

        lax.fori_loop(0, rows // BLOCK, body, 0)

    def receive(step):
        @pl.when(has_prev)
        def _():
            halo(step, 0).wait_recv()

        @pl.when(has_next)
        def _():
            halo(step, 1).wait_recv()

        part = jnp.concatenate([halves(yrecv[step, side]) for side in range(2)], axis=0)
        for s in range(0, rows, BLOCK):
            at = slice(s, s + BLOCK)
            a[step, at] = (folded(dot(scat[at], part)) + loc[at]) * (1.0 / UNIT)

    pl.semaphore_wait(barrier, n - 1)
    precondition(b_ref, w.at[0])
    for step in range(STEPS):
        send(step)
        if step == 0:
            build()
        local()
        receive(step)
        if step + 1 < STEPS:
            precondition(a.at[step], w.at[step + 1])

    b = b_ref[...]
    iid = jnp.broadcast_to(iid_ref[...], (8, rows))

    def scaled(value):
        return jnp.dot(iid, value, precision=lax.Precision.HIGHEST, preferred_element_type=F32)[:1]

    ba = [column_sum(b * a[k]) for k in range(3)]
    bw = [b * w[k] for k in range(3)]
    lines = [
        column_sum(bw[0]),
        column_sum(bw[1]),
        column_sum(a[0] * w[1]),
        column_sum(a[1] * w[1]),
        column_sum(a[1] * w[2]),
        column_sum(a[2] * w[2]),
        column_sum(b * b) - ba[0] - scaled(bw[0]),
        ba[0] - ba[1] - scaled(bw[1]),
        ba[1] - ba[2] - scaled(bw[2]),
    ]
    lines = lines + [jnp.zeros_like(lines[0])] * (STATS - len(lines))
    stats[...] = jnp.concatenate(lines, axis=0)

    def tell(k):
        other = lax.rem(me + k, n)
        return pltpu.make_async_remote_copy(
            src_ref=stats,
            dst_ref=gathered.at[k],
            send_sem=stat_send.at[k],
            recv_sem=stat_recv.at[k],
            device_id=device(other),
            device_id_type=MESH,
        )

    def start_tell(k, carry):
        tell(k).start()
        return carry

    def wait_tell(k, carry):
        tell(k).wait_recv()
        return carry

    lax.fori_loop(1, n, start_tell, 0)
    gathered[0] = stats[...]
    lax.fori_loop(1, n, wait_tell, 0)
    sums = jnp.sum(gathered[...], axis=0)
    m = [sums[k : k + 1] for k in range(9)]

    d = [m[k] - m[k + 1] for k in range(5)]

    def inverse_pivot(pivot, diagonal):
        usable = pivot > TINY * diagonal
        return jnp.where(usable, 1.0 / jnp.where(usable, pivot, 1.0), 0.0)

    i0 = inverse_pivot(d[0], d[0])
    l10, l20 = d[1] * i0, d[2] * i0
    i1 = inverse_pivot(d[2] - l10 * d[1], d[2])
    e21 = d[3] - l20 * d[1]
    l21 = e21 * i1
    i2 = inverse_pivot(d[4] - l20 * d[2] - l21 * e21, d[4])
    y0 = m[0]
    y1 = m[1] - l10 * y0
    y2 = m[2] - l20 * y0 - l21 * y1
    c2 = y2 * i2
    c1 = y1 * i1 - l21 * c2
    c0 = y0 * i0 - l10 * c1 - l20 * c2
    x_ref[...] = c0 * w[0] + c1 * w[1] + c2 * w[2]
    trace_ref[...] = (c0 * m[6] + c1 * m[7] + c2 * m[8]) / (n * rows)

    for step in range(STEPS):
        @pl.when(has_next)
        def _():
            halo(step, 0).wait_send()

        @pl.when(has_prev)
        def _():
            halo(step, 1).wait_send()

    def end_tell(k, carry):
        tell(k).wait_send()
        return carry

    lax.fori_loop(1, n, end_tell, 0)


def on_device(region, inner, probes, neighbours, lengths, iid_precision, send_rows):
    rows, width = probes.shape
    bound = send_rows.shape[1]
    n = region * inner
    vmem = pl.BlockSpec(memory_space=pltpu.VMEM)
    x, trace = pl.pallas_call(
        functools.partial(kernel, region, inner),
        out_shape=(
            jax.ShapeDtypeStruct((rows, width), F32),
            jax.ShapeDtypeStruct((1, width), F32),
        ),
        in_specs=[vmem] * 5,
        out_specs=(vmem, vmem),
        scratch_shapes=[
            pltpu.VMEM((rows, rows), BF16),
            pltpu.VMEM((rows, rows), BF16),
            pltpu.VMEM((2 * bound, rows), BF16),
            pltpu.VMEM((2 * bound, rows), BF16),
            pltpu.VMEM((rows, 2 * bound), BF16),
            pltpu.VMEM((rows, BLOCK), BF16),
            pltpu.VMEM((rows, BLOCK), BF16),
            pltpu.VMEM((neighbours.shape[1], rows), F32),
            pltpu.VMEM((rows, 2 * width), BF16),
            pltpu.VMEM((rows, width), F32),
            pltpu.VMEM((STEPS, rows, width), F32),
            pltpu.VMEM((STEPS, rows, width), F32),
            pltpu.VMEM((STEPS, 2, bound, width), F32),
            pltpu.VMEM((STEPS, 2, bound, width), F32),
            pltpu.VMEM((STATS, width), F32),
            pltpu.VMEM((n, STATS, width), F32),
            pltpu.SemaphoreType.DMA((STEPS, 2)),
            pltpu.SemaphoreType.DMA((STEPS, 2)),
            pltpu.SemaphoreType.DMA((n,)),
            pltpu.SemaphoreType.DMA((n,)),
        ],
        compiler_params=pltpu.CompilerParams(
            collective_id=0, has_side_effects=True, vmem_limit_bytes=48 * 2**20
        ),
        name="trace_gradient",
    )(neighbours.T, lengths.T, iid_precision.reshape(1, rows), send_rows, probes)
    return x, trace.reshape(width)


def solution(mesh):
    return jax.shard_map(
        functools.partial(on_device, mesh.shape["region"], mesh.shape["sub"]),
        mesh=mesh,
        in_specs=(
            P(("region", "sub"), None),
            P(("region", "sub"), None),
            P(("region", "sub"), None),
            P(("region", "sub")),
            P(("region", "sub"), None),
        ),
        out_specs=(P(("region", "sub"), None), P()),
        check_vma=False,
    )
```

time: 557 us -> 39.7 us (0.07)
  blocking collectives: 240 us -> 0 us
  local copies, waits for them, and re-layouts: 154 us -> 5.22 us
  other arithmetic: 120 us -> 0 us
  Pallas kernels: 0 us -> 33.4 us
  starting transfers between devices: 25.5 us -> 0 us
  matrix products: 12.1 us -> 0 us
    psum x6 -> x0, blocking collectives: 240 us -> none  [the longest x3 119 us: residual_norm(): return lax.psum(jnp.sum(residual * precond, axis=0), ('region', 'sub'))]
    gather x40 -> x0, local copies, waits for them, and re-layouts: 139 us -> none  [the longest x32 130 us: apply_rows(): total = total - weights[:, slot, None] * extended[neighbours[:, slot]]]
    another operation x7 -> x0, other arithmetic: 94.8 us -> none  [the longest x4 94.1 us: block_inverses(): factor = jnp.linalg.cholesky(blocks)]
    pallas_call x0 -> x1, Pallas kernels: none -> 33.4 us  [on_device(): pl.pallas_call(functools.partial(kernel, region, inner), out_shape=(jax.S...]
    ppermute x8 -> x0, starting transfers between devices: 25.5 us -> none  [passed_along(): return lax.ppermute(shard, axis, pairs)]
    reduce_sum x5 -> x0, other arithmetic: 17.1 us -> none  [the longest x3 12.5 us: direction_curvature(): terms = (jnp.sum(direction * image, axis=0),)]
    dot_general x3 -> x0, matrix products: 9.95 us -> none  [precondition(): jnp.einsum('gij,gjp->gip', inverse, grouped, precision=lax.Precision.HIGH...]
  transfers between devices with their start and end apart: 8 -> 0, of which waited for: 0 -> 0; matrix products, arithmetic and copies ran while one was open for 17% -> 0% of each run, Pallas kernels for 0% -> 0%
where the time goes in v1:
time: 39.7 us; the launch traced here: 39.3 us
  Pallas kernels  33.4 us (84%)
  local copies, waits for them, and re-layouts  5.22 us (13%)
  between operations  0.65 us (2%)
    pallas_call x1, Pallas kernels, on_device(): pl.pallas_call(functools.partial(kernel, region, inner), out_shape=(jax.S...  33.4 us
    unnamed x12, local copies, waits for them, and re-layouts  5.22 us

profile of v1, /device:TPU:15, one launch (start us, length us, event | category | flops | bytes accessed | tf_op | source)
XLA Modules:
  0.0 39.3 jit_solution(17724870534031575445)
XLA Ops:
  0.6 0.0 copy-start.3
  0.6 0.7 %copy-done.3 = f32[1024]{0:T(1024)S(1)} copy-done((f32[1024]{0:T(1024)S(1)}, f32[1024]{0:T(1024)}, u32[]{:S(2)}) %copy-start.3) | copy-done | bytes 4120
  1.3 0.0 copy-start
  1.3 1.0 %copy-done = f32[1024,128]{1,0:T(8,128)S(1)} copy-done((f32[1024,128]{1,0:T(8,128)S(1)}, f32[1024,128]{1,0:T(8,128)}, u32[]{:S(2)}) %copy-start) | copy-done | bytes 524312
  2.4 0.0 copy-start.1
  2.4 0.8 %copy-done.1 = s32[1024,8]{0,1:T(8,128)S(1)} copy-done((s32[1024,8]{0,1:T(8,128)S(1)}, s32[1024,8]{0,1:T(8,128)}, u32[]{:S(2)}) %copy-start.1) | copy-done | bytes 32792
  3.1 0.0 copy-start.2
  3.1 0.8 %copy-done.2 = s32[1024,8]{0,1:T(8,128)S(1)} copy-done((s32[1024,8]{0,1:T(8,128)S(1)}, s32[1024,8]{0,1:T(8,128)}, u32[]{:S(2)}) %copy-start.2) | copy-done | bytes 32792
  3.9 0.0 copy-start.4
  3.9 0.7 %copy-done.4 = s32[2,256]{1,0:T(2,128)S(1)} copy-done((s32[2,256]{1,0:T(2,128)S(1)}, s32[2,256]{1,0:T(2,128)}, u32[]{:S(2)}) %copy-start.4) | copy-done | bytes 2072
  4.6 33.4 %trace_gradient.1 = (f32[1024,128]{1,0:T(8,128)S(1)}, f32[1,128]{1,0:T(1,128)S(1)}) custom-call(s32[8,1024]{1,0:T(8,128)S(1)} %bitcast.4, s32[8,1024]{1,0:T(8,128)S(1)} %bitcast.5, f32[1,1024]{1,0:T(1,128)S(1)} %bitcast.6, s32[2,256]{1,0:T(2,128)S(1)} %copy-done.4, f32[1024,128]{1,0:T(8,128)S(1)} %copy-done), custom_call_target="tpu_custom_call" | custom-call | tf_op jit(solution)/shard_map/trace_gradient/pallas_call | solution.py:301
  38.0 0.8 %copy.9 = f32[1024,128]{1,0:T(8,128)} copy(f32[1024,128]{1,0:T(8,128)S(1)} %get-tuple-element.8) | data formatting | bytes 1048576
  38.8 0.5 %copy.10 = f32[128]{0:T(128)} copy(f32[128]{0:T(128)S(1)} %bitcast.7) | data formatting | bytes 1024
Async XLA Ops:
  0.6 0.7 %copy-start.3 = (f32[1024]{0:T(1024)S(1)}, f32[1024]{0:T(1024)}, u32[]{:S(2)}) copy-start(f32[1024]{0:T(1024)} %param.8) | copy-start | bytes 12292
  1.3 1.0 %copy-start = (f32[1024,128]{1,0:T(8,128)S(1)}, f32[1024,128]{1,0:T(8,128)}, u32[]{:S(2)}) copy-start(f32[1024,128]{1,0:T(8,128)} %b_ref.1) | copy-start | bytes 1572868
  2.4 0.8 %copy-start.1 = (s32[1024,8]{0,1:T(8,128)S(1)}, s32[1024,8]{0,1:T(8,128)}, u32[]{:S(2)}) copy-start(s32[1024,8]{0,1:T(8,128)} %param.6) | copy-start | bytes 98308
  3.1 0.8 %copy-start.2 = (s32[1024,8]{0,1:T(8,128)S(1)}, s32[1024,8]{0,1:T(8,128)}, u32[]{:S(2)}) copy-start(s32[1024,8]{0,1:T(8,128)} %param.7) | copy-start | bytes 98308
  3.9 0.7 %copy-start.4 = (s32[2,256]{1,0:T(2,128)S(1)}, s32[2,256]{1,0:T(2,128)}, u32[]{:S(2)}) copy-start(s32[2,256]{1,0:T(2,128)} %send_ref.1) | copy-start | bytes 6148
